TPU v7x, 32 devices: a whole 2x2x4 slice. The times are simulated.
32 devices in a mesh: grp: 2 (over x), reg: 16 (over z, y, core).
Axes of the slice: x: 2, y: 2, z: 4, core: 2. Of those that a mesh axis runs over, the one named last changes fastest.
Arguments:
- expect_marks: float32 [256, 256, 16, 2], P(('grp', 'reg')), parts along dimension 0, may hold values from -6 to 6
- policy_resp: bfloat16 [256, 256, 2, 128], P(('grp', 'reg')), parts along dimension 0, may hold values from -0.0029296875 to 0.0029296875
- lottery_weight: float32 [256, 256], P('grp'), parts along dimension 0, may hold values from 0 to 1
- lottery_index: int32 [256, 256], P('grp'), parts along dimension 0, may hold values from 0 to 254, as said below
- migration_weight: float32 [256, 4], P('grp'), parts along dimension 0, may hold values from 0.2 to 5
- neighbours: int32 [256, 4], P('grp'), parts along dimension 0, may hold values from 0 to 127, as said below
Outputs:
- jacobian: float32 [256, 2, 2, 128], P(('grp', 'reg')), parts along dimension 0
There are 2 independent parts, one for each index of `grp`. A program takes and returns all parts, laid end to end along the dimension named above; each array names one. Nothing has to cross between parts.
Inputs may be any that keep to these rules, and one draw needn't show every extreme that they name: `lottery_index`: each point's lower bracket lies within 2 points of it; the first point's is 0 and the last point's is 254. `neighbours`: every destination lies within 2 regions of its own region; the first entry of each list is the region itself.
All inputs are finite; a program needn't handle non-finite values.
Results may differ from a plain program's by a relative error of at most 0.0029.
Values sent between devices are 32-bit elements; how exact they have to be, the bound alone decides.
A program may use at most 128 MiB of HBM per device.

v0:
```python
import jax
import jax.numpy as jnp
from jax import lax
from jax.sharding import PartitionSpec as P

REACH = 2
H = 8


def padded_2(cells, sides, width):
    for axis, dim in sides:
        count = lax.axis_size(axis)
        ends = count - 1
        head = lax.slice_in_dim(cells, 0, width, axis=dim)
        tail = lax.slice_in_dim(cells, cells.shape[dim] - width, cells.shape[dim], axis=dim)
        cells = jnp.concatenate(
            [
                lax.ppermute(tail, axis, [(i, (i + 1) % count) for i in range(ends)]),
                cells,
                lax.ppermute(head, axis, [((i + 1) % count, i) for i in range(ends)]),
            ],
            axis=dim,
        )
    return cells


def entering(array, axis, combine, identity):
    length, place = (lax.axis_size(axis), lax.axis_index(axis))
    everything = jax.tree.map(lambda part: lax.all_gather(part, axis), array)
    start = jax.tree.map(
        lambda part, zero: jnp.broadcast_to(jnp.asarray(zero, part.dtype), part.shape),
        array,
        identity,
    )

    def step(k, before):
        reached = k < place
        new = combine(before, jax.tree.map(lambda part: part[k], everything))
        return jax.tree.map(lambda a, b: jnp.where(reached, a, b), new, before)

    return lax.fori_loop(0, length, step, start)


def shift_right(values, amount):
    return jnp.pad(values[:, :, :-amount], ((0, 0), (0, 0), (amount, 0)))


def shift_traced(values, amount):
    columns = lax.broadcasted_iota(jnp.int32, values.shape, 2)
    rolled = jnp.roll(values, amount, axis=2)
    return jnp.where(columns >= amount, rolled, jnp.zeros_like(values))


def combine(earlier, later):
    return (shift_traced(earlier[0], later[1]) + later[0], earlier[1] + later[1])


def shift_points(field, offset):
    padded = jnp.pad(field, ((0, 0), (3, 3), (0, 0)))
    return padded[:, 3 + offset : 3 + offset + field.shape[1], :]


def advance(state_field, base_in, base_out, count_out, tables):
    pad_mix, pad_targets, pad_omega, pad_index, margin = tables
    weights = lax.dynamic_slice_in_dim(pad_mix, base_out + margin, count_out, 0)
    targets = lax.dynamic_slice_in_dim(pad_targets, base_out + margin, count_out, 0)
    sources = base_in + jnp.arange(state_field.shape[0], dtype=jnp.int32)
    matrix = jnp.sum(weights[:, :, None] * (targets[:, :, None] == sources[None, None, :]), axis=1)
    mixed_field = jnp.dot(
        matrix, state_field.reshape(state_field.shape[0], -1), precision=lax.Precision.HIGHEST
    )
    mixed_field = mixed_field.reshape(count_out, state_field.shape[1], state_field.shape[2])
    omega_rows = lax.dynamic_slice_in_dim(pad_omega, base_out + margin, count_out, 0)[:, :, None]
    bracket = lax.dynamic_slice_in_dim(pad_index, base_out + margin, count_out, 0)
    points_here = jnp.arange(mixed_field.shape[1], dtype=jnp.int32)[None, :]
    offset_of = (bracket - points_here)[:, :, None]
    shifted = [shift_points(mixed_field, offset) for offset in range(-2, 4)]
    below_side = jnp.zeros_like(mixed_field)
    above_side = jnp.zeros_like(mixed_field)
    for offset in range(-2, 3):
        picked = offset_of == offset
        below_side = below_side + jnp.where(picked, shifted[offset + 2], 0.0)
        above_side = above_side + jnp.where(picked, shifted[offset + 3], 0.0)
    return omega_rows * below_side + (1.0 - omega_rows) * above_side


def per_device(
    expect_marks, policy_resp, lottery_weight, lottery_index, migration_weight, neighbours
):
    regions, points, checkpoints, outcomes = expect_marks.shape
    shocks = policy_resp.shape[2]
    length = policy_resp.shape[3]
    reach_rows = REACH
    block_base = lax.axis_index("reg") * regions
    rows_owned = length // lax.axis_size("reg")
    group_steps = min(H - 1, regions // reach_rows)
    margin = group_steps * reach_rows
    mix_weights = migration_weight / jnp.sum(migration_weight, axis=1, keepdims=True)
    pad_mix = jnp.pad(mix_weights, ((margin, margin), (0, 0)))
    pad_targets = jnp.pad(neighbours, ((margin, margin), (0, 0)), constant_values=-1)
    pad_omega = jnp.pad(lottery_weight, ((margin, margin), (0, 0)))
    pad_index = jnp.pad(lottery_index, ((margin, margin), (0, 0)))
    tables = (pad_mix, pad_targets, pad_omega, pad_index, margin)
    state_field = expect_marks.reshape(regions, points, checkpoints * outcomes)
    stored = [state_field.astype(jnp.bfloat16)]
    for horizon in range(1, H):
        extended = padded_2(state_field, (("reg", 0),), reach_rows)
        state_field = advance(extended, block_base - reach_rows, block_base, regions, tables)
        stored.append(state_field.astype(jnp.bfloat16))
    pieces = [piece.reshape(regions, points, checkpoints, outcomes) for piece in stored]
    expect_all = jnp.stack(pieces, axis=3).reshape(regions * points, length * outcomes)
    flat_policy = policy_resp.reshape(regions * points, shocks * length)
    partial_news = lax.dot_general(
        expect_all, flat_policy, (((0,), (0,)), ((), ())), preferred_element_type=jnp.float32
    )
    summed = lax.psum(partial_news, "reg")
    own_news = lax.dynamic_slice_in_dim(
        summed, lax.axis_index("reg") * rows_owned * outcomes, rows_owned * outcomes, 0
    )
    own_news = own_news.reshape(rows_owned, outcomes, shocks, length)
    previous = jnp.zeros((outcomes, shocks, length), jnp.float32)
    rows_local = []
    for row_index in range(rows_owned):
        previous = own_news[row_index] + shift_right(previous, 1)
        rows_local.append(previous)
    identity = (jnp.zeros((outcomes, shocks, length), jnp.float32), jnp.zeros((), jnp.int32))
    summary = (previous, jnp.full((), rows_owned, jnp.int32))
    carry_in, ignored = entering(summary, "reg", combine, identity)
    finished = [
        rows_local[row_index] + shift_right(carry_in, row_index + 1)
        for row_index in range(rows_owned)
    ]
    return jnp.stack(finished, axis=0)


def solution(mesh):
    return jax.shard_map(
        per_device,
        mesh=mesh,
        in_specs=(
            P(("grp", "reg"), None, None, None),
            P(("grp", "reg"), None, None, None),
            P("grp", None),
            P("grp", None),
            P("grp", None),
            P("grp", None),
        ),
        out_specs=P(("grp", "reg"), None, None, None),
        check_vma=False,
    )
```

profile of v0, /device:TPU:0, one launch (start us, length us, event | category | flops | bytes accessed | tf_op | source)
XLA Modules:
  0.0 280.6 jit_solution(1973947087554414350)
XLA Ops:
  6.5 0.9 fusion.112
  7.6 2.4 collective-permute-start
  10.2 1.3 collective-permute-start.1
  11.5 5.8 %copy.73 = f32[8,256,16,2]{0,3,2,1:T(2,128)} copy(f32[8,256,16,2]{1,3,2,0:T(2,128)} %param.8) | data formatting | bytes 524288 | tf_op args[0]
  17.6 2.8 %copy.75 = f32[8,8192]{1,0:T(8,128)S(1)} copy(f32[8,8192]{0,1:T(8,128)} %bitcast.109) | data formatting | bytes 524288 | tf_op jit(solution)/shard_map/concatenate | solution.py:16
  21.5 0.7 copy.76
  23.1 5.2 %collective-permute-start.2 = (f32[2,256,32]{1,0,2:T(2,128)S(1)}, f32[2,256,32]{1,0,2:T(2,128)S(1)}, u32[]{:S(2)}, u32[]{:S(2)}) collective-permute-start(f32[2,256,32]{1,0,2:T(2,128)S(1)} %get-tuple-element.202), channel_id=1, source_target_pairs={{0,1},{1,2},{2,3},{3,4},{4,5},{5,6},{6,7},{7,8},{8,9},{9,10},{10,1... | collective-permute-start | bytes 196616 | tf_op jit(solution)/shard_map/ppermute | solution.py:18
  28.3 1.3 collective-permute-start.3
  29.7 3.0 %collective-permute-done.3 = f32[2,256,32]{1,0,2:T(2,128)S(1)} collective-permute-done((f32[2,256,32]{1,0,2:T(2,128)S(1)}, f32[2,256,32]{1,0,2:T(2,128)S(1)}, u32[]{:S(2)}, u32[]{:S(2)}) %collective-permute-start.3) | collective-permute-done | bytes 65568 | tf_op jit(solution)/shard_map/ppermute | solution.py:20
  33.3 0.7 reshape.85
  34.5 0.7 copy.78
  36.1 4.8 %collective-permute-start.4 = (f32[2,256,32]{1,0,2:T(2,128)S(1)}, f32[2,256,32]{1,0,2:T(2,128)S(1)}, u32[]{:S(2)}, u32[]{:S(2)}) collective-permute-start(f32[2,256,32]{1,0,2:T(2,128)S(1)} %get-tuple-element.200), channel_id=1, source_target_pairs={{0,1},{1,2},{2,3},{3,4},{4,5},{5,6},{6,7},{7,8},{8,9},{9,10},{10,1... | collective-permute-start | bytes 196616 | tf_op jit(solution)/shard_map/ppermute | solution.py:18
  40.9 1.3 collective-permute-start.5
  42.4 1.7 collective-permute-done.5
  44.7 0.7 reshape.86
  45.9 0.7 copy.80
  47.5 6.0 %collective-permute-start.6 = (f32[2,256,32]{1,0,2:T(2,128)S(1)}, f32[2,256,32]{1,0,2:T(2,128)S(1)}, u32[]{:S(2)}, u32[]{:S(2)}) collective-permute-start(f32[2,256,32]{1,0,2:T(2,128)S(1)} %get-tuple-element.198), channel_id=1, source_target_pairs={{0,1},{1,2},{2,3},{3,4},{4,5},{5,6},{6,7},{7,8},{8,9},{9,10},{10,1... | collective-permute-start | bytes 196616 | tf_op jit(solution)/shard_map/ppermute | solution.py:18
  53.6 1.5 collective-permute-start.7
  55.2 1.5 collective-permute-done.7
  57.3 0.7 reshape.87
  58.6 0.7 copy.82
  60.1 5.3 %collective-permute-start.8 = (f32[2,256,32]{1,0,2:T(2,128)S(1)}, f32[2,256,32]{1,0,2:T(2,128)S(1)}, u32[]{:S(2)}, u32[]{:S(2)}) collective-permute-start(f32[2,256,32]{1,0,2:T(2,128)S(1)} %get-tuple-element.196), channel_id=1, source_target_pairs={{0,1},{1,2},{2,3},{3,4},{4,5},{5,6},{6,7},{7,8},{8,9},{9,10},{10,1... | collective-permute-start | bytes 196616 | tf_op jit(solution)/shard_map/ppermute | solution.py:18
  65.4 1.3 collective-permute-start.9
  66.8 1.7 collective-permute-done.9
  69.2 0.7 reshape.88
  70.4 0.7 copy.84
  72.0 5.3 %collective-permute-start.10 = (f32[2,256,32]{1,0,2:T(2,128)S(1)}, f32[2,256,32]{1,0,2:T(2,128)S(1)}, u32[]{:S(2)}, u32[]{:S(2)}) collective-permute-start(f32[2,256,32]{1,0,2:T(2,128)S(1)} %get-tuple-element.194), channel_id=1, source_target_pairs={{0,1},{1,2},{2,3},{3,4},{4,5},{5,6},{6,7},{7,8},{8,9},{9,10},{10,1... | collective-permute-start | bytes 196616 | tf_op jit(solution)/shard_map/ppermute | solution.py:18
  77.2 1.3 collective-permute-start.11
  78.7 1.7 collective-permute-done.11
  81.0 0.7 reshape.89
  82.3 0.7 copy.86
  83.8 5.3 %collective-permute-start.12 = (f32[2,256,32]{1,0,2:T(2,128)S(1)}, f32[2,256,32]{1,0,2:T(2,128)S(1)}, u32[]{:S(2)}, u32[]{:S(2)}) collective-permute-start(f32[2,256,32]{1,0,2:T(2,128)S(1)} %get-tuple-element.192), channel_id=1, source_target_pairs={{0,1},{1,2},{2,3},{3,4},{4,5},{5,6},{6,7},{7,8},{8,9},{9,10},{10,1... | collective-permute-start | bytes 196616 | tf_op jit(solution)/shard_map/ppermute | solution.py:18
  89.1 1.5 collective-permute-start.13
  90.7 1.5 collective-permute-done.13
  92.8 0.7 reshape.90
  94.1 0.7 copy.88
  95.7 1.1 copy.96
  97.2 0.9 copy-done.6
  98.1 1.2 fusion.4
  99.9 0.8 dynamic-update-slice
  100.6 14.3 %all-reduce.27 = s32[16]{0:T(128)S(1)} all-reduce(s32[16]{0:T(128)S(1)} %dynamic-update-slice), channel_id=1, replica_groups=mesh['grp'=2,'reg'=16] {'reg'}, use_global_device_ids=true, to_apply=%add.27 | all-reduce | flops 16 | bytes 128
  115.0 77.4 %all-reduce.30.cloned.1.call-done = f32[256,256]{1,0:T(8,128)} async-done(((f32[256,256]{1,0:T(8,128)}), f32[256,256]{1,0:T(8,128)}) %all-reduce.30.cloned.1.call-update) | async-done | bytes 262160 | tf_op jit(solution)/shard_map/psum | solution.py:116
  192.4 0.9 constant_dynamic-slice_fusion.6
  194.0 20.9 %all-gather = f32[32,2,128]{2,1,0:T(2,128)S(1)} all-gather(f32[2,2,128]{2,1,0:T(2,128)S(1)} %pad_add_fusion), channel_id=2, replica_groups=mesh['grp'=2,'reg'=16] {'reg'}, dimensions={0}, use_global_device_ids=true | all-gather | bytes 34816 | tf_op jit(solution)/shard_map/all_gather | solution.py:29
  214.9 57.0 %while.16 = (s32[]{:T(128)}, f32[2,2,128]{2,1,0:T(2,128)S(1)}, s32[]{:T(128)}, s32[16]{0:T(128)S(1)}, f32[16,2,2,128]{3,2,1,0:T(2,128)S(1)}, /*index=5*/s32[]{:T(128)}, s32[]{:T(128)}, s32[]{:T(128)}, s32[]{:T(128)}, s32[]{:T(128)}) while((s32[]{:T(128)}, f32[2,2,128]{2,1,0:T(2,128)S(1)}, s32[]{:T(128)}, s32[16]{0:T(128)S(1)}, ...), condition=%wide.region_4.5_spmd.clone, body=%wide.region_3.4_spmd.clone.sunk | while | flops 2707 | bytes 10796 | solution.py:41
  217.6 0.7 iota_compare_fusion.2
  224.8 0.7 iota_compare_fusion.2
  231.9 0.7 iota_compare_fusion.2
  (179 shorter events, 39.6 us)
Async XLA Ops:
  6.5 185.9 %all-reduce.30.cloned.1.call-start = ((), (), s32[]{:S(2)}) async-start(), calls=%async_computation | async-start | bytes 524288 | tf_op jit(solution)/shard_map/psum | solution.py:116
  7.6 13.0 %collective-permute-start = (f32[2,256,32]{2,1,0:T(8,128)S(1)}, f32[2,256,32]{2,1,0:T(8,128)S(1)}, u32[]{:S(2)}, u32[]{:S(2)}) collective-permute-start(f32[2,256,32]{2,1,0:T(8,128)S(1)} %copy.72), channel_id=1, source_target_pairs={{0,1},{1,2},{2,3},{3,4},{4,5},{5,6},{6,7},{7,8},{8,9},{9,10},{10,1... | collective-permute-start | bytes 196616 | tf_op jit(solution)/shard_map/ppermute | solution.py:18
  10.2 10.6 %collective-permute-start.1 = (f32[2,256,32]{2,1,0:T(8,128)S(1)}, f32[2,256,32]{2,1,0:T(8,128)S(1)}, u32[]{:S(2)}, u32[]{:S(2)}) collective-permute-start(f32[2,256,32]{2,1,0:T(8,128)S(1)} %copy.74), channel_id=1, source_target_pairs={{1,0},{2,1},{3,2},{4,3},{5,4},{6,5},{7,6},{8,7},{9,8},{10,9},{11,1... | collective-permute-start | bytes 196616 | tf_op jit(solution)/shard_map/ppermute | solution.py:20
  11.5 5.8 %copy-start = (f32[8,256,16,2]{1,3,2,0:T(2,128)S(1)}, f32[8,256,16,2]{1,3,2,0:T(2,128)}, u32[]{:S(2)}) copy-start(f32[8,256,16,2]{1,3,2,0:T(2,128)} %param.8) | copy-start | bytes 786436
  11.5 5.9 %copy-start.3 = (f32[128,4]{0,1:T(4,128)S(1)}, f32[128,4]{0,1:T(4,128)}, u32[]{:S(2)}) copy-start(f32[128,4]{0,1:T(4,128)} %param.12) | copy-start | bytes 6148
  11.5 6.0 %copy-start.4 = (s32[128,4]{0,1:T(4,128)S(1)}, s32[128,4]{0,1:T(4,128)}, u32[]{:S(2)}) copy-start(s32[128,4]{0,1:T(4,128)} %param.13) | copy-start | bytes 6148
  17.6 2.8 %copy-start.2 = (s32[128,256]{1,0:T(8,128)S(1)}, s32[128,256]{1,0:T(8,128)}, u32[]{:S(2)}) copy-start(s32[128,256]{1,0:T(8,128)} %param.11) | copy-start | bytes 393220
  17.6 3.0 %copy-start.1 = (f32[128,256]{1,0:T(8,128)S(1)}, f32[128,256]{1,0:T(8,128)}, u32[]{:S(2)}) copy-start(f32[128,256]{1,0:T(8,128)} %param.10) | copy-start | bytes 393220
  23.1 6.6 %collective-permute-start.2 = (f32[2,256,32]{1,0,2:T(2,128)S(1)}, f32[2,256,32]{1,0,2:T(2,128)S(1)}, u32[]{:S(2)}, u32[]{:S(2)}) collective-permute-start(f32[2,256,32]{1,0,2:T(2,128)S(1)} %get-tuple-element.202), channel_id=1, source_target_pairs={{0,1},{1,2},{2,3},{3,4},{4,5},{5,6},{6,7},{7,8},{8,9},{9,10},{10,1... | collective-permute-start | bytes 196616 | tf_op jit(solution)/shard_map/ppermute | solution.py:18
  28.3 4.4 %collective-permute-start.3 = (f32[2,256,32]{1,0,2:T(2,128)S(1)}, f32[2,256,32]{1,0,2:T(2,128)S(1)}, u32[]{:S(2)}, u32[]{:S(2)}) collective-permute-start(f32[2,256,32]{1,0,2:T(2,128)S(1)} %get-tuple-element.203), channel_id=1, source_target_pairs={{1,0},{2,1},{3,2},{4,3},{5,4},{6,5},{7,6},{8,7},{9,8},{10,9},{11,1... | collective-permute-start | bytes 196616 | tf_op jit(solution)/shard_map/ppermute | solution.py:20
  36.1 6.3 %collective-permute-start.4 = (f32[2,256,32]{1,0,2:T(2,128)S(1)}, f32[2,256,32]{1,0,2:T(2,128)S(1)}, u32[]{:S(2)}, u32[]{:S(2)}) collective-permute-start(f32[2,256,32]{1,0,2:T(2,128)S(1)} %get-tuple-element.200), channel_id=1, source_target_pairs={{0,1},{1,2},{2,3},{3,4},{4,5},{5,6},{6,7},{7,8},{8,9},{9,10},{10,1... | collective-permute-start | bytes 196616 | tf_op jit(solution)/shard_map/ppermute | solution.py:18
  40.9 3.1 %collective-permute-start.5 = (f32[2,256,32]{1,0,2:T(2,128)S(1)}, f32[2,256,32]{1,0,2:T(2,128)S(1)}, u32[]{:S(2)}, u32[]{:S(2)}) collective-permute-start(f32[2,256,32]{1,0,2:T(2,128)S(1)} %get-tuple-element.201), channel_id=1, source_target_pairs={{1,0},{2,1},{3,2},{4,3},{5,4},{6,5},{7,6},{8,7},{9,8},{10,9},{11,1... | collective-permute-start | bytes 196616 | tf_op jit(solution)/shard_map/ppermute | solution.py:20
  47.5 7.7 %collective-permute-start.6 = (f32[2,256,32]{1,0,2:T(2,128)S(1)}, f32[2,256,32]{1,0,2:T(2,128)S(1)}, u32[]{:S(2)}, u32[]{:S(2)}) collective-permute-start(f32[2,256,32]{1,0,2:T(2,128)S(1)} %get-tuple-element.198), channel_id=1, source_target_pairs={{0,1},{1,2},{2,3},{3,4},{4,5},{5,6},{6,7},{7,8},{8,9},{9,10},{10,1... | collective-permute-start | bytes 196616 | tf_op jit(solution)/shard_map/ppermute | solution.py:18
  53.6 3.1 %collective-permute-start.7 = (f32[2,256,32]{1,0,2:T(2,128)S(1)}, f32[2,256,32]{1,0,2:T(2,128)S(1)}, u32[]{:S(2)}, u32[]{:S(2)}) collective-permute-start(f32[2,256,32]{1,0,2:T(2,128)S(1)} %get-tuple-element.199), channel_id=1, source_target_pairs={{1,0},{2,1},{3,2},{4,3},{5,4},{6,5},{7,6},{8,7},{9,8},{10,9},{11,1... | collective-permute-start | bytes 196616 | tf_op jit(solution)/shard_map/ppermute | solution.py:20
  60.1 6.7 %collective-permute-start.8 = (f32[2,256,32]{1,0,2:T(2,128)S(1)}, f32[2,256,32]{1,0,2:T(2,128)S(1)}, u32[]{:S(2)}, u32[]{:S(2)}) collective-permute-start(f32[2,256,32]{1,0,2:T(2,128)S(1)} %get-tuple-element.196), channel_id=1, source_target_pairs={{0,1},{1,2},{2,3},{3,4},{4,5},{5,6},{6,7},{7,8},{8,9},{9,10},{10,1... | collective-permute-start | bytes 196616 | tf_op jit(solution)/shard_map/ppermute | solution.py:18
  65.4 3.1 %collective-permute-start.9 = (f32[2,256,32]{1,0,2:T(2,128)S(1)}, f32[2,256,32]{1,0,2:T(2,128)S(1)}, u32[]{:S(2)}, u32[]{:S(2)}) collective-permute-start(f32[2,256,32]{1,0,2:T(2,128)S(1)} %get-tuple-element.197), channel_id=1, source_target_pairs={{1,0},{2,1},{3,2},{4,3},{5,4},{6,5},{7,6},{8,7},{9,8},{10,9},{11,1... | collective-permute-start | bytes 196616 | tf_op jit(solution)/shard_map/ppermute | solution.py:20
  72.0 6.7 %collective-permute-start.10 = (f32[2,256,32]{1,0,2:T(2,128)S(1)}, f32[2,256,32]{1,0,2:T(2,128)S(1)}, u32[]{:S(2)}, u32[]{:S(2)}) collective-permute-start(f32[2,256,32]{1,0,2:T(2,128)S(1)} %get-tuple-element.194), channel_id=1, source_target_pairs={{0,1},{1,2},{2,3},{3,4},{4,5},{5,6},{6,7},{7,8},{8,9},{9,10},{10,1... | collective-permute-start | bytes 196616 | tf_op jit(solution)/shard_map/ppermute | solution.py:18
  77.2 3.1 %collective-permute-start.11 = (f32[2,256,32]{1,0,2:T(2,128)S(1)}, f32[2,256,32]{1,0,2:T(2,128)S(1)}, u32[]{:S(2)}, u32[]{:S(2)}) collective-permute-start(f32[2,256,32]{1,0,2:T(2,128)S(1)} %get-tuple-element.195), channel_id=1, source_target_pairs={{1,0},{2,1},{3,2},{4,3},{5,4},{6,5},{7,6},{8,7},{9,8},{10,9},{11,1... | collective-permute-start | bytes 196616 | tf_op jit(solution)/shard_map/ppermute | solution.py:20
  83.8 6.9 %collective-permute-start.12 = (f32[2,256,32]{1,0,2:T(2,128)S(1)}, f32[2,256,32]{1,0,2:T(2,128)S(1)}, u32[]{:S(2)}, u32[]{:S(2)}) collective-permute-start(f32[2,256,32]{1,0,2:T(2,128)S(1)} %get-tuple-element.192), channel_id=1, source_target_pairs={{0,1},{1,2},{2,3},{3,4},{4,5},{5,6},{6,7},{7,8},{8,9},{9,10},{10,1... | collective-permute-start | bytes 196616 | tf_op jit(solution)/shard_map/ppermute | solution.py:18
  89.1 3.1 %collective-permute-start.13 = (f32[2,256,32]{1,0,2:T(2,128)S(1)}, f32[2,256,32]{1,0,2:T(2,128)S(1)}, u32[]{:S(2)}, u32[]{:S(2)}) collective-permute-start(f32[2,256,32]{1,0,2:T(2,128)S(1)} %get-tuple-element.193), channel_id=1, source_target_pairs={{1,0},{2,1},{3,2},{4,3},{5,4},{6,5},{7,6},{8,7},{9,8},{10,9},{11,1... | collective-permute-start | bytes 196616 | tf_op jit(solution)/shard_map/ppermute | solution.py:20
  96.8 1.2 copy-start.6
  97.2 2.1 copy-start.7
  272.5 0.6 copy-start.5
Sparse Core Ops, SparseCore 0:
  99.4 92.9 all-reduce.29
where the time goes:
time: 282 us; the launch traced here: 281 us
  waiting for transfers between devices  88.6 us (31%)
  starting transfers between devices  43.6 us (15%)
  local copies, waits for them, and re-layouts  43.4 us (15%)
  blocking collectives  35.2 us (12%)
  loops' own time  33.8 us (12%)
  other arithmetic  18.1 us (6%)
  between operations  14.1 us (5%)
  matrix products  3.8 us (1%)
    psum x1, waiting for transfers between devices, per_device(): summed = lax.psum(partial_news, 'reg')  77.4 us
    ppermute x7, starting transfers between devices, padded_2(): lax.ppermute(tail, axis, [(i, (i + 1) % count) for i in range(ends)])  34.2 us
    another operation x1, loops' own time, entering(): return lax.fori_loop(0, length, step, start)  33.8 us
    all_gather x1, blocking collectives, entering(): everything = jax.tree.map(lambda part: lax.all_gather(part, axis), array)  20.9 us
    unnamed x1, blocking collectives  14.3 us
    ppermute x7, waiting for transfers between devices, padded_2(): lax.ppermute(head, axis, [((i + 1) % count, i) for i in range(ends)])  11.2 us
    ge x16, other arithmetic, shift_traced(): return jnp.where(columns >= amount, rolled, jnp.zeros_like(values))  11.1 us
    dynamic_slice x16, local copies, waits for them, and re-layouts, step(): new = combine(before, jax.tree.map(lambda part: part[k], everything))  10.7 us
  transfers between devices with their start and end apart: 15, of which 7 were waited for; matrix products, arithmetic and copies ran while one was open for 4% of the time, Pallas kernels for 0%

commit v1 on v0

v1 whole, which is shorter than its diff:
```python
import functools
import jax
import jax.numpy as jnp
from jax import lax
from jax.experimental import pallas as pl
from jax.experimental.pallas import tpu as pltpu
from jax.sharding import PartitionSpec as P

REACH = 2
H = 8
FIRST = 4


def kernel(n, e_ref, pol_hbm, lw_ref, li_ref, mw_ref, nb_ref, out_ref,
           x0, x1, x2, eb, pol, acc, coef, wb, wt, jp, ra, sb, rb,
           psem, hsend, hrecv, asem, bsend, brecv):
    regions, cols, points = e_ref.shape
    length = pol.shape[2] // 2
    chips = n // 2
    d = lax.axis_index("reg")
    par = lax.rem(d, 2)
    chip = lax.div(d, 2)
    sib = d + 1 - 2 * par

    policy_copy = pltpu.make_async_copy(pol_hbm, pol, psem)
    policy_copy.start()

    barrier = pltpu.get_barrier_semaphore()

    def greet(other):
        pl.semaphore_signal(barrier, inc=1, device_id={"reg": other},
                            device_id_type=pl.DeviceIdType.MESH)

    @pl.when(d > 0)
    def _():
        greet(d - 1)

    @pl.when(d < n - 1)
    def _():
        greet(d + 1)

    for off in range(1, chips):
        greet(2 * lax.rem(chip + off, chips) + par)
    ends = jnp.where(d > 0, 1, 0) + jnp.where(d < n - 1, 1, 0)
    pl.semaphore_wait(barrier, ends + (chips - 1))

    def halo(stage, to_left):
        if stage == 0:
            src = e_ref
            buf, width = x0, regions
            lo = 0
        else:
            width = (H - 1 - FIRST) * REACH
            lo = regions if to_left else 2 * regions - width
            src = x2.at[pl.ds(lo, width)]
            buf = x2
        dst = buf.at[pl.ds(2 * regions if to_left else regions - width, width)]
        side = 0 if to_left else 1
        return pltpu.make_async_remote_copy(
            src_ref=src, dst_ref=dst,
            send_sem=hsend.at[stage, side], recv_sem=hrecv.at[stage, side],
            device_id={"reg": d - 1 if to_left else d + 1},
            device_id_type=pl.DeviceIdType.MESH)

    def start_halo(stage):
        @pl.when(d > 0)
        def _():
            halo(stage, True).start()

        @pl.when(d < n - 1)
        def _():
            halo(stage, False).start()

    def wait_halo(stage):
        @pl.when(d > 0)
        def _():
            halo(stage, True).wait_send()
            halo(stage, False).wait_recv()

        @pl.when(d < n - 1)
        def _():
            halo(stage, False).wait_send()
            halo(stage, True).wait_recv()

    start_halo(0)

    mw = mw_ref[...]
    mix = mw / jnp.sum(mw, axis=0, keepdims=True)
    offs = nb_ref[...] - lax.broadcasted_iota(jnp.int32, mw.shape, 1)
    rows = [jnp.sum(jnp.where(offs == o, mix, 0.0), axis=0, keepdims=True)
            for o in range(-REACH, REACH + 1)]
    rows.append(jnp.zeros((8 - len(rows), mw.shape[1]), jnp.float32))
    wt[...] = jnp.transpose(jnp.concatenate(rows, axis=0))

    lane = lax.broadcasted_iota(jnp.int32, (regions, points), 1)
    for b in range(3):
        g = d - 1 + b
        valid = jnp.logical_and(g >= 0, g < n)
        at = pl.ds(pl.multiple_of(jnp.clip(g, 0, n - 1) * regions, regions), regions)
        here = pl.ds(b * regions, regions)
        om = lw_ref[at, :]
        off = li_ref[at, :] - lane
        for o in range(-REACH, REACH + 2):
            c = jnp.where(off == o, om, 0.0) + jnp.where(off == o - 1, 1.0 - om, 0.0)
            coef[o + REACH, here, :] = jnp.where(valid, c, 0.0)
        w = wt[at, :]
        for o in range(2 * REACH + 1):
            wb[o, here, :] = jnp.broadcast_to(w[:, o:o + 1], (regions, points))

    def own(r, _):
        x = e_ref[r]
        x0[regions + r] = x
        eb[r, 0:cols, :] = x.astype(jnp.bfloat16)
        return 0

    lax.fori_loop(0, regions, own, 0)
    zeros = jnp.zeros((cols, points), jnp.float32)

    def clear(first):
        def one(r, _):
            x0[first + r] = zeros
            x2[first + r] = zeros
            return 0
        lax.fori_loop(0, regions, one, 0)

    @pl.when(d == 0)
    def _():
        clear(0)

    @pl.when(d == n - 1)
    def _():
        clear(2 * regions)

    def region(src, dst, r, j, keep):
        m = wb[0, pl.ds(r, 1), :] * src[r - REACH]
        for o in range(1, 2 * REACH + 1):
            m = m + wb[o, pl.ds(r, 1), :] * src[r - REACH + o]
        out = coef[REACH, pl.ds(r, 1), :] * m
        for o in range(-REACH, REACH + 2):
            if o != 0:
                out = out + coef[o + REACH, pl.ds(r, 1), :] * pltpu.roll(
                    m, (-o) % points, 1)
        dst[r] = out
        if keep:
            eb[r - regions, pl.ds(j * cols, cols), :] = out.astype(jnp.bfloat16)

    def advance(src, dst, j, extra):
        def halo_one(i, _):
            region(src, dst, regions - extra + i, j, False)
            region(src, dst, 2 * regions + i, j, False)
            return 0

        def own_one(i, _):
            region(src, dst, regions + i, j, True)
            return 0

        if extra:
            lax.fori_loop(0, extra, halo_one, 0)
        lax.fori_loop(0, regions, own_one, 0)

    def dots(lo, hi):
        tile = min(256, 2 * length)

        def one(i, _):
            r = lax.div(i, 2 * length // tile)
            t = pl.ds(pl.multiple_of(lax.rem(i, 2 * length // tile) * tile, tile), tile)
            p = jnp.dot(eb[r, lo * cols:hi * cols, :], pol[r, :, t],
                        preferred_element_type=jnp.float32)
            acc[lo * cols:hi * cols, t] += p
            return 0

        lax.fori_loop(0, regions * (2 * length // tile), one, 0)

    acc[...] = jnp.zeros_like(acc)
    wait_halo(0)
    bufs = [x0, x1]
    for j in range(1, FIRST):
        advance(bufs[(j - 1) % 2], bufs[j % 2], j, REACH * (FIRST - j))
    advance(bufs[(FIRST - 1) % 2], x2, FIRST, 0)
    start_halo(1)
    policy_copy.wait()
    dots(0, FIRST + 1)
    wait_halo(1)
    src = x2
    for j in range(FIRST + 1, H):
        dst = bufs[j % 2]
        advance(src, dst, j, REACH * (H - 1 - j))
        src = dst
    dots(FIRST + 1, H)

    width = 2 * length
    pos = lax.rem(lax.broadcasted_iota(jnp.int32, (cols, width), 1), length)
    row = lax.broadcasted_iota(jnp.int32, (cols, width), 0)

    def later(x, amount):
        return jnp.where(pos >= amount, pltpu.roll(x, amount, 1), 0.0)

    prev = acc[0:cols, :]
    for j in range(1, H):
        prev = acc[j * cols:(j + 1) * cols, :] + later(prev, 1)
        acc[j * cols:(j + 1) * cols, :] = prev
    step = 1
    while 2 * step < cols:
        moved = pltpu.roll(later(prev, H * step), 2 * step, 0)
        prev = prev + jnp.where(row >= 2 * step, moved, 0.0)
        step *= 2
    carry = jnp.where(row >= 2, pltpu.roll(prev, 2, 0), 0.0)
    for j in range(H):
        v = acc[j * cols:(j + 1) * cols, :] + later(carry, j + 1)
        jp[:, :, j] = v.reshape(chips, 2, 2, width)

    pair = pltpu.make_async_remote_copy(
        src_ref=jp.at[:, 1 - par], dst_ref=ra, send_sem=asem.at[0], recv_sem=asem.at[1],
        device_id={"reg": sib}, device_id_type=pl.DeviceIdType.MESH)
    pair.start()
    pair.wait()

    def part(off):
        q = lax.rem(chip + off, chips)
        return pltpu.make_async_remote_copy(
            src_ref=sb.at[off], dst_ref=rb.at[off],
            send_sem=bsend.at[off], recv_sem=brecv.at[off],
            device_id={"reg": 2 * q + par}, device_id_type=pl.DeviceIdType.MESH)

    for off in range(1, chips):
        q = lax.rem(chip + off, chips)
        sb[off] = jp[q, par] + ra[q]
        part(off).start()
    total = jp[chip, par] + ra[chip]
    for off in range(1, chips):
        part(off).wait()
        total = total + rb[off]
    out_ref[...] = total


def per_device(
    expect_marks, policy_resp, lottery_weight, lottery_index, migration_weight, neighbours
):
    n = lax.axis_size("reg")
    regions, points, marks, outcomes = expect_marks.shape
    shocks, length = policy_resp.shape[2:]
    cols = marks * outcomes
    assert marks == n and outcomes == 2 and shocks == 2 and length == n * H
    assert regions >= REACH * FIRST and regions % 8 == 0
    field = jnp.transpose(expect_marks, (0, 2, 3, 1)).reshape(regions, cols, points)
    policy = policy_resp.reshape(regions, points, shocks * length)
    f32 = jnp.float32
    slab = pltpu.VMEM((3 * regions, cols, points), f32)
    vmem = pl.BlockSpec(memory_space=pltpu.VMEM)
    width = shocks * length
    got = pl.pallas_call(
        functools.partial(kernel, n),
        out_shape=jax.ShapeDtypeStruct((H, outcomes, width), f32),
        in_specs=[vmem, pl.BlockSpec(memory_space=pl.ANY), vmem, vmem, vmem, vmem],
        out_specs=vmem,
        scratch_shapes=[
            slab, slab, slab,
            pltpu.VMEM((regions, H * cols, points), jnp.bfloat16),
            pltpu.VMEM((regions, points, width), jnp.bfloat16),
            pltpu.VMEM((H * cols, width), f32),
            pltpu.VMEM((2 * REACH + 2, 3 * regions, points), f32),
            pltpu.VMEM((2 * REACH + 1, 3 * regions, points), f32),
            pltpu.VMEM((regions * n, 8), f32),
            pltpu.VMEM((n // 2, 2, H, 2, width), f32),
            pltpu.VMEM((n // 2, H, 2, width), f32),
            pltpu.VMEM((n // 2, H, 2, width), f32),
            pltpu.VMEM((n // 2, H, 2, width), f32),
            pltpu.SemaphoreType.DMA,
            pltpu.SemaphoreType.DMA((2, 2)),
            pltpu.SemaphoreType.DMA((2, 2)),
            pltpu.SemaphoreType.DMA((2,)),
            pltpu.SemaphoreType.DMA((n // 2,)),
            pltpu.SemaphoreType.DMA((n // 2,)),
        ],
        compiler_params=pltpu.CompilerParams(
            collective_id=0, has_side_effects=True, vmem_limit_bytes=56 * 2**20),
        name="jacobian",
    )(field, policy, lottery_weight, lottery_index,
      jnp.transpose(migration_weight), jnp.transpose(neighbours))
    return got.reshape(H, outcomes, shocks, length)


def solution(mesh):
    return jax.shard_map(
        per_device,
        mesh=mesh,
        in_specs=(
            P(("grp", "reg"), None, None, None),
            P(("grp", "reg"), None, None, None),
            P("grp", None),
            P("grp", None),
            P("grp", None),
            P("grp", None),
        ),
        out_specs=P(("grp", "reg"), None, None, None),
        check_vma=False,
    )
```

time: 282 us -> 42.4 us (0.15)
  waiting for transfers between devices: 88.6 us -> 0 us
  starting transfers between devices: 43.6 us -> 0 us
  local copies, waits for them, and re-layouts: 43.4 us -> 5.72 us
  Pallas kernels: 0 us -> 36.4 us
  blocking collectives: 35.2 us -> 0 us
  loops' own time: 33.8 us -> 0 us
  other arithmetic: 18.1 us -> 0 us
  between operations: 14.1 us -> 0.01 us
  matrix products: 3.8 us -> 0 us
    psum x1 -> x0, waiting for transfers between devices: 77.4 us -> none  [per_device(): summed = lax.psum(partial_news, 'reg')]
    ppermute x14 -> x0, starting transfers between devices: 43.6 us -> none  [the longest x7 34.2 us: padded_2(): lax.ppermute(tail, axis, [(i, (i + 1) % count) for i in range(ends)])]
    pallas_call x0 -> x1, Pallas kernels: none -> 36.4 us  [per_device(): pl.pallas_call(functools.partial(kernel, n), out_shape=jax.ShapeDtypeStru...]
    another operation x1 -> x0, loops' own time: 33.8 us -> none  [entering(): return lax.fori_loop(0, length, step, start)]
    all_gather x1 -> x0, blocking collectives: 20.9 us -> none  [entering(): everything = jax.tree.map(lambda part: lax.all_gather(part, axis), array)]
    unnamed x1 -> x0, blocking collectives: 14.3 us -> none
    ppermute x14 -> x0, waiting for transfers between devices: 11.2 us -> none  [the longest x7 11.2 us: padded_2(): lax.ppermute(head, axis, [((i + 1) % count, i) for i in range(ends)])]
    ge x16 -> x0, other arithmetic: 11.1 us -> none  [shift_traced(): return jnp.where(columns >= amount, rolled, jnp.zeros_like(values))]
  transfers between devices with their start and end apart: 15 -> 0, of which waited for: 7 -> 0; matrix products, arithmetic and copies ran while one was open for 4% -> 0% of each run, Pallas kernels for 0% -> 0%
where the time goes in v1:
time: 42.4 us; the launch traced here: 42.2 us
  Pallas kernels  36.4 us (86%)
  local copies, waits for them, and re-layouts  5.72 us (13%)
    pallas_call x1, Pallas kernels, per_device(): pl.pallas_call(functools.partial(kernel, n), out_shape=jax.ShapeDtypeStru...  36.4 us
    reshape x1, local copies, waits for them, and re-layouts, per_device(): policy = policy_resp.reshape(regions, points, shocks * length)  2.53 us
    reshape x1, local copies, waits for them, and re-layouts, per_device(): jnp.transpose(expect_marks, (0, 2, 3, 1)).reshape(regions, cols, points)  1.85 us
    reshape x1, local copies, waits for them, and re-layouts, per_device(): return got.reshape(H, outcomes, shocks, length)  1.35 us

profile of v1, /device:TPU:0, one launch (start us, length us, event | category | flops | bytes accessed | tf_op | source)
XLA Modules:
  0.0 42.2 jit_solution(5625072589093204292)
XLA Ops:
  0.0 1.8 %reshape.9.e_ref = f32[8,32,256]{2,1,0:T(8,128)} reshape(f32[8,16,2,256]{3,2,1,0:T(2,128)} %bitcast.3) | data formatting | bytes 524288 | tf_op jit(solution)/shard_map/reshape | solution.py:245
  1.8 2.5 %reshape.10.pol_hbm = bf16[8,256,256]{2,1,0:T(8,128)(2,1)} reshape(bf16[8,256,2,128]{3,2,1,0:T(2,128)(2,1)} %param.7) | data formatting | bytes 2097152 | tf_op jit(solution)/shard_map/reshape | solution.py:246
  4.4 36.4 %jacobian.1 = f32[8,2,256]{2,1,0:T(2,128)} custom-call(f32[8,32,256]{2,1,0:T(8,128)} %reshape.9.e_ref, bf16[8,256,256]{2,1,0:T(8,128)(2,1)} %reshape.10.pol_hbm, f32[128,256]{1,0:T(8,128)} %lw_ref.1, s32[128,256]{1,0:T(8,128)} %li_ref.1, f32[4,128]{1,0:T(4,128)} %bitcast.4, s32[4,128]{1,0:T(4,128)} %bitcast.5), custom_call_target="tpu_custom_call" | custom-call | tf_op jit(solution)/shard_map/jacobian/pallas_call | solution.py:251
  40.8 1.3 %reshape.11 = f32[8,2,2,128]{3,2,1,0:T(2,128)} reshape(f32[8,2,256]{2,1,0:T(2,128)} %jacobian.1) | data formatting | bytes 32768 | tf_op jit(solution)/shard_map/reshape | solution.py:280

commit v2 on v1

v2 whole, which is shorter than its diff:
```python
import functools
import jax
import jax.numpy as jnp
from jax import lax
from jax.experimental import pallas as pl
from jax.experimental.pallas import tpu as pltpu
from jax.sharding import PartitionSpec as P

REACH = 2
H = 8
FIRST = 4


def kernel(n, e_hbm, pol_hbm, lw_hbm, li_hbm, mw_hbm, nb_hbm, out_ref,
           x0, x1, x2, x3, x4, ebuf, pbuf, pf, lwb, lib, mwb, nbb,
           eb, pol, acc, coef, wb, wt, jp, ra, sb, rb,
           isem, hsend, hrecv, asem, bsend, brecv):
    regions, marks, _, points = ebuf.shape
    cols = 2 * marks
    length = pol.shape[2] // 2
    chips = n // 2
    d = lax.axis_index("reg")
    par = lax.rem(d, 2)
    chip = lax.div(d, 2)
    sib = d + 1 - 2 * par

    barrier = pltpu.get_barrier_semaphore()

    def greet(other):
        pl.semaphore_signal(barrier, inc=1, device_id={"reg": other},
                            device_id_type=pl.DeviceIdType.MESH)

    @pl.when(d > 0)
    def _():
        greet(d - 1)

    @pl.when(d < n - 1)
    def _():
        greet(d + 1)

    for off in range(1, chips):
        greet(2 * lax.rem(chip + off, chips) + par)

    def table_rows(b):
        g = jnp.clip(d - 1 + b, 0, n - 1) * regions
        return pl.ds(pl.multiple_of(g, regions), regions)

    loads = [(e_hbm, ebuf), (mw_hbm, mwb), (nb_hbm, nbb)]
    for b in range(3):
        here = pl.ds(b * regions, regions)
        loads.append((lw_hbm.at[table_rows(b)], lwb.at[here]))
        loads.append((li_hbm.at[table_rows(b)], lib.at[here]))
    loads.append((pol_hbm, pbuf))
    loads = [pltpu.make_async_copy(a, v, isem.at[q]) for q, (a, v) in enumerate(loads)]
    for c in loads:
        c.start()

    loads[0].wait()

    def own(r, _):
        x = ebuf[r].reshape(cols, points)
        x0[regions + r] = x
        eb[r, 0:cols, :] = x.astype(jnp.bfloat16)
        return 0

    lax.fori_loop(0, regions, own, 0)

    for c in loads[1:-1]:
        c.wait()
    mw = mwb[...]
    mix = mw / jnp.sum(mw, axis=0, keepdims=True)
    offs = nbb[...] - lax.broadcasted_iota(jnp.int32, mw.shape, 1)
    rows = [jnp.sum(jnp.where(offs == o, mix, 0.0), axis=0, keepdims=True)
            for o in range(-REACH, REACH + 1)]
    rows.append(jnp.zeros((8 - len(rows), mw.shape[1]), jnp.float32))
    wt[...] = jnp.transpose(jnp.concatenate(rows, axis=0))

    lane = lax.broadcasted_iota(jnp.int32, (regions, points), 1)
    for b in range(3):
        g = d - 1 + b
        valid = jnp.logical_and(g >= 0, g < n)
        here = pl.ds(b * regions, regions)
        om = lwb[here, :]
        off = lib[here, :] - lane
        for o in range(-REACH, REACH + 2):
            c = jnp.where(off == o, om, 0.0) + jnp.where(off == o - 1, 1.0 - om, 0.0)
            coef[o + REACH, here, :] = jnp.where(valid, c, 0.0)
        w = wt[table_rows(b), :]
        for o in range(2 * REACH + 1):
            wb[o, here, :] = jnp.broadcast_to(w[:, o:o + 1], (regions, points))

    zeros = jnp.zeros((cols, points), jnp.float32)

    def clear(first):
        def one(r, _):
            x0[first + r] = zeros
            x4[first + r] = zeros
            return 0
        lax.fori_loop(0, regions, one, 0)

    @pl.when(d == 0)
    def _():
        clear(0)

    @pl.when(d == n - 1)
    def _():
        clear(2 * regions)

    ends = jnp.where(d > 0, 1, 0) + jnp.where(d < n - 1, 1, 0)
    pl.semaphore_wait(barrier, ends + (chips - 1))

    def halo(stage, to_left, c):
        buf = x4 if stage else x0
        near = c * REACH
        if to_left:
            src, dst = regions + near, 2 * regions + near
        else:
            src, dst = 2 * regions - near - REACH, regions - near - REACH
        side = 0 if to_left else 1
        return pltpu.make_async_remote_copy(
            src_ref=buf.at[pl.ds(src, REACH)], dst_ref=buf.at[pl.ds(dst, REACH)],
            send_sem=hsend.at[stage, side, c], recv_sem=hrecv.at[stage, side, c],
            device_id={"reg": d - 1 if to_left else d + 1},
            device_id_type=pl.DeviceIdType.MESH)

    def start_halo(stage, chunks):
        @pl.when(d > 0)
        def _():
            for c in chunks:
                halo(stage, True, c).start()

        @pl.when(d < n - 1)
        def _():
            for c in chunks:
                halo(stage, False, c).start()

    def wait_halo(stage, c):
        @pl.when(d > 0)
        def _():
            halo(stage, False, c).wait_recv()

        @pl.when(d < n - 1)
        def _():
            halo(stage, True, c).wait_recv()

    def sent_halo(stage, chunks):
        @pl.when(d > 0)
        def _():
            for c in chunks:
                halo(stage, True, c).wait_send()

        @pl.when(d < n - 1)
        def _():
            for c in chunks:
                halo(stage, False, c).wait_send()

    chunks0 = range(FIRST)
    chunks1 = range(H - 1 - FIRST)
    start_halo(0, chunks0)

    loads[-1].wait()

    def split_shocks(r, _):
        v = pbuf[pl.ds(pl.multiple_of(r * 2 * points, 2 * points), 2 * points), :]
        v = v.astype(jnp.float32)
        for t in range(length // 128):
            pf[t] = v[:, t * 128:(t + 1) * 128]
        for t in range(length // 128):
            for i in range(2):
                at = i * length + t * 128
                pol[r, :, at:at + 128] = pf[t, pl.ds(i, points, stride=2), :].astype(
                    jnp.bfloat16)
        return 0

    lax.fori_loop(0, regions, split_shocks, 0)

    def piece(src, dst, r, j, keep, sl):
        m = wb[0, pl.ds(r, 1), :] * src[r - REACH, sl, :]
        for o in range(1, 2 * REACH + 1):
            m = m + wb[o, pl.ds(r, 1), :] * src[r - REACH + o, sl, :]
        out = coef[REACH, pl.ds(r, 1), :] * m
        for o in range(-REACH, REACH + 2):
            if o != 0:
                out = out + coef[o + REACH, pl.ds(r, 1), :] * pltpu.roll(
                    m, (-o) % points, 1)
        dst[r, sl, :] = out
        if keep:
            return out.astype(jnp.bfloat16)

    def several(src, dst, which, j, keep):
        def block(i, _):
            c0 = pl.multiple_of(i * 32, 32)
            for r in which:
                kept = piece(src, dst, r, j, keep, pl.ds(c0, 32))
                if keep:
                    eb[r - regions, pl.ds(j * cols + c0, 32), :] = kept
            return 0

        if cols == 32:
            block(0, 0)
        else:
            lax.fori_loop(0, cols // 32, block, 0)

    def ring(src, dst, c, j):
        near = c * REACH
        lo, hi = regions - near - REACH, 2 * regions + near
        several(src, dst, [lo + q for q in range(REACH)] + [hi + q for q in range(REACH)],
                j, False)

    def inner(src, dst, j, start=0):
        def one(i, _):
            several(src, dst, [regions + start + 4 * i + q for q in range(4)], j, True)
            return 0
        lax.fori_loop(0, (regions - 2 * start) // 4, one, 0)

    def edge(src, dst, j):
        several(src, dst, [regions, regions + 1, 2 * regions - 2, 2 * regions - 1], j, True)

    def dots(lo, hi):
        tile = min(256, 2 * length)

        def one(i, _):
            r = lax.div(i, 2 * length // tile)
            t = pl.ds(pl.multiple_of(lax.rem(i, 2 * length // tile) * tile, tile), tile)
            p = jnp.dot(eb[r, lo * cols:hi * cols, :], pol[r, :, t],
                        preferred_element_type=jnp.float32)
            acc[lo * cols:hi * cols, t] += p
            return 0

        lax.fori_loop(0, regions * (2 * length // tile), one, 0)

    acc[...] = jnp.zeros_like(acc)
    first = [x0, x1, x2, x3, x4]
    for c in chunks0:
        wait_halo(0, c)
        for j in range(1, c + 1):
            ring(first[j - 1], first[j], c - j, j)
        if c + 1 < FIRST:
            inner(first[c], first[c + 1], c + 1)
        else:
            edge(first[c], first[c + 1], c + 1)
            start_halo(1, [0])
            inner(first[c], first[c + 1], c + 1, REACH)
            start_halo(1, chunks1[1:])
    dots(0, FIRST + 1)
    second = [x4, x1, x2, x3]
    for c in chunks1:
        wait_halo(1, c)
        for j in range(1, c + 1):
            ring(second[j - 1], second[j], c - j, FIRST + j)
        inner(second[c], second[c + 1], FIRST + c + 1)
    dots(FIRST + 1, H)
    sent_halo(0, chunks0)
    sent_halo(1, chunks1)

    width = 2 * length
    pos = lax.rem(lax.broadcasted_iota(jnp.int32, (cols, width), 1), length)
    row = lax.broadcasted_iota(jnp.int32, (cols, width), 0)

    def later(x, amount):
        return jnp.where(pos >= amount, pltpu.roll(x, amount, 1), 0.0)

    prev = acc[0:cols, :]
    for j in range(1, H):
        prev = acc[j * cols:(j + 1) * cols, :] + later(prev, 1)
        acc[j * cols:(j + 1) * cols, :] = prev
    step = 1
    while 2 * step < cols:
        moved = pltpu.roll(later(prev, H * step), 2 * step, 0)
        prev = prev + jnp.where(row >= 2 * step, moved, 0.0)
        step *= 2
    carry = jnp.where(row >= 2, pltpu.roll(prev, 2, 0), 0.0)
    for j in range(H):
        v = acc[j * cols:(j + 1) * cols, :] + later(carry, j + 1)
        jp[:, :, j] = v.reshape(chips, 2, 2, width)

    pair = pltpu.make_async_remote_copy(
        src_ref=jp.at[:, 1 - par], dst_ref=ra, send_sem=asem.at[0], recv_sem=asem.at[1],
        device_id={"reg": sib}, device_id_type=pl.DeviceIdType.MESH)
    pair.start()
    pair.wait()

    def part(off):
        q = lax.rem(chip + off, chips)
        return pltpu.make_async_remote_copy(
            src_ref=sb.at[off], dst_ref=rb.at[off],
            send_sem=bsend.at[off], recv_sem=brecv.at[off],
            device_id={"reg": 2 * q + par}, device_id_type=pl.DeviceIdType.MESH)

    for off in range(1, chips):
        q = lax.rem(chip + off, chips)
        sb[off] = jp[q, par] + ra[q]
        part(off).start()
    total = jp[chip, par] + ra[chip]
    for off in range(1, chips):
        part(off).wait()
        total = total + rb[off]
    for i in range(2):
        out_ref[:, :, i, :] = total[:, :, i * length:(i + 1) * length]


def per_device(
    expect_marks, policy_resp, lottery_weight, lottery_index, migration_weight, neighbours
):
    n = lax.axis_size("reg")
    regions, points, marks, outcomes = expect_marks.shape
    shocks, length = policy_resp.shape[2:]
    cols = marks * outcomes
    assert marks == n and outcomes == 2 and shocks == 2 and length == n * H
    assert regions >= REACH * FIRST and regions % 8 == 0
    field = jnp.transpose(expect_marks, (0, 2, 3, 1))
    policy = policy_resp.reshape(regions * points * shocks, length)
    f32 = jnp.float32
    slab = pltpu.VMEM((3 * regions, cols, points), f32)
    width = shocks * length
    entries = neighbours.shape[1]
    return pl.pallas_call(
        functools.partial(kernel, n),
        out_shape=jax.ShapeDtypeStruct((H, outcomes, shocks, length), f32),
        in_specs=[pl.BlockSpec(memory_space=pl.ANY)] * 6,
        out_specs=pl.BlockSpec(memory_space=pltpu.VMEM),
        scratch_shapes=[
            slab, slab, slab, slab, slab,
            pltpu.VMEM((regions, marks, outcomes, points), f32),
            pltpu.VMEM((regions * points * shocks, length), jnp.bfloat16),
            pltpu.VMEM((length // 128, shocks * points, 128), f32),
            pltpu.VMEM((3 * regions, points), f32),
            pltpu.VMEM((3 * regions, points), jnp.int32),
            pltpu.VMEM((entries, regions * n), f32),
            pltpu.VMEM((entries, regions * n), jnp.int32),
            pltpu.VMEM((regions, H * cols, points), jnp.bfloat16),
            pltpu.VMEM((regions, points, width), jnp.bfloat16),
            pltpu.VMEM((H * cols, width), f32),
            pltpu.VMEM((2 * REACH + 2, 3 * regions, points), f32),
            pltpu.VMEM((2 * REACH + 1, 3 * regions, points), f32),
            pltpu.VMEM((regions * n, 8), f32),
            pltpu.VMEM((n // 2, 2, H, 2, width), f32),
            pltpu.VMEM((n // 2, H, 2, width), f32),
            pltpu.VMEM((n // 2, H, 2, width), f32),
            pltpu.VMEM((n // 2, H, 2, width), f32),
            pltpu.SemaphoreType.DMA((10,)),
            pltpu.SemaphoreType.DMA((2, 2, FIRST)),
            pltpu.SemaphoreType.DMA((2, 2, FIRST)),
            pltpu.SemaphoreType.DMA((2,)),
            pltpu.SemaphoreType.DMA((n // 2,)),
            pltpu.SemaphoreType.DMA((n // 2,)),
        ],
        compiler_params=pltpu.CompilerParams(
            collective_id=0, has_side_effects=True, vmem_limit_bytes=56 * 2**20),
        name="jacobian",
    )(field, policy, lottery_weight, lottery_index,
      jnp.transpose(migration_weight), jnp.transpose(neighbours))


def solution(mesh):
    return jax.shard_map(
        per_device,
        mesh=mesh,
        in_specs=(
            P(("grp", "reg"), None, None, None),
            P(("grp", "reg"), None, None, None),
            P("grp", None),
            P("grp", None),
            P("grp", None),
            P("grp", None),
        ),
        out_specs=P(("grp", "reg"), None, None, None),
        check_vma=False,
    )
```

time: 42.4 us -> 29.7 us (0.70)
  Pallas kernels: 36.4 us -> 28.2 us
  local copies, waits for them, and re-layouts: 5.72 us -> 1.32 us
    pallas_call x1, Pallas kernels: 36.4 us -> 28.2 us  [per_device(): pl.pallas_call(functools.partial(kernel, n), out_shape=jax.ShapeDtypeStru...]
    reshape x3 -> x0, local copies, waits for them, and re-layouts: 5.72 us -> none  [the longest x1 2.53 us: per_device(): policy = policy_resp.reshape(regions, points, shocks * length)]
    unnamed x0 -> x1, local copies, waits for them, and re-layouts: none -> 1.32 us
where the time goes in v2:
time: 29.7 us; the launch traced here: 29.5 us
  Pallas kernels  28.2 us (95%)
  local copies, waits for them, and re-layouts  1.32 us (4%)
    pallas_call x1, Pallas kernels, per_device(): pl.pallas_call(functools.partial(kernel, n), out_shape=jax.ShapeDtypeStru...  28.2 us
    unnamed x1, local copies, waits for them, and re-layouts  1.32 us

profile of v2, /device:TPU:0, one launch (start us, length us, event | category | flops | bytes accessed | tf_op | source)
XLA Modules:
  0.0 29.5 jit_solution(9904325277265430171)
XLA Ops:
  0.0 28.2 %jacobian.1 = f32[8,2,2,128]{3,2,1,0:T(2,128)} custom-call(f32[8,16,2,256]{3,2,1,0:T(2,128)} %bitcast.5, bf16[4096,128]{1,0:T(8,128)(2,1)} %bitcast.4, f32[128,256]{1,0:T(8,128)} %lw_hbm.1, s32[128,256]{1,0:T(8,128)} %li_hbm.1, f32[4,128]{1,0:T(4,128)} %bitcast.6, s32[4,128]{1,0:T(4,128)} %bitcast.7), custom_call_target="tpu_custom_call" | custom-call | tf_op jit(solution)/shard_map/jacobian/pallas_call | solution.py:317
  28.2 1.3 %copy.8 = f32[8,2,2,128]{3,2,1,0:T(2,128)} copy(f32[8,2,2,128]{3,2,1,0:T(2,128)} %jacobian.1) | data formatting | bytes 32768

commit v3 on v2

--- a/solution.py
+++ b/solution.py
@@ -38,9 +38,6 @@
     def _():
         greet(d + 1)
 
-    for off in range(1, chips):
-        greet(2 * lax.rem(chip + off, chips) + par)
-
     def table_rows(b):
         g = jnp.clip(d - 1 + b, 0, n - 1) * regions
         return pl.ds(pl.multiple_of(g, regions), regions)
@@ -55,6 +52,9 @@
     for c in loads:
         c.start()
 
+    for off in range(1, chips):
+        greet(2 * lax.rem(chip + off, chips) + par)
+
     loads[0].wait()
 
     def own(r, _):
@@ -64,6 +64,61 @@
         return 0
 
     lax.fori_loop(0, regions, own, 0)
+
+    ends = jnp.where(d > 0, 1, 0) + jnp.where(d < n - 1, 1, 0)
+    pl.semaphore_wait(barrier, ends + (chips - 1))
+
+    def halo(stage, to_left, c, part):
+        some = pl.ds(part * (cols // 2), cols // 2)
+        buf = x4 if stage else x0
+        near = c * REACH
+        if to_left:
+            src, dst = regions + near, 2 * regions + near
+        else:
+            src, dst = 2 * regions - near - REACH, regions - near - REACH
+        side = 0 if to_left else 1
+        return pltpu.make_async_remote_copy(
+            src_ref=buf.at[pl.ds(src, REACH), some], dst_ref=buf.at[pl.ds(dst, REACH), some],
+            send_sem=hsend.at[stage, side, c, part],
+            recv_sem=hrecv.at[stage, side, c, part],
+            device_id={"reg": d - 1 if to_left else d + 1},
+            device_id_type=pl.DeviceIdType.MESH)
+
+    def start_halo(stage, chunks, part):
+        @pl.when(d > 0)
+        def _():
+            for c in chunks:
+                halo(stage, True, c, part).start()
+
+        @pl.when(d < n - 1)
+        def _():
+            for c in chunks:
+                halo(stage, False, c, part).start()
+
+    def wait_halo(stage, c, part):
+        @pl.when(d > 0)
+        def _():
+            halo(stage, False, c, part).wait_recv()
+
+        @pl.when(d < n - 1)
+        def _():
+            halo(stage, True, c, part).wait_recv()
+
+    def sent_halo(stage, chunks, part):
+        @pl.when(d > 0)
+        def _():
+            for c in chunks:
+                halo(stage, True, c, part).wait_send()
+
+        @pl.when(d < n - 1)
+        def _():
+            for c in chunks:
+                halo(stage, False, c, part).wait_send()
+
+    chunks0 = range(FIRST)
+    chunks1 = range(H - 1 - FIRST)
+    start_halo(0, chunks0, 0)
+    start_halo(0, chunks0, 1)
 
     for c in loads[1:-1]:
         c.wait()
@@ -106,58 +161,6 @@
     def _():
         clear(2 * regions)
 
-    ends = jnp.where(d > 0, 1, 0) + jnp.where(d < n - 1, 1, 0)
-    pl.semaphore_wait(barrier, ends + (chips - 1))
-
-    def halo(stage, to_left, c):
-        buf = x4 if stage else x0
-        near = c * REACH
-        if to_left:
-            src, dst = regions + near, 2 * regions + near
-        else:
-            src, dst = 2 * regions - near - REACH, regions - near - REACH
-        side = 0 if to_left else 1
-        return pltpu.make_async_remote_copy(
-            src_ref=buf.at[pl.ds(src, REACH)], dst_ref=buf.at[pl.ds(dst, REACH)],
-            send_sem=hsend.at[stage, side, c], recv_sem=hrecv.at[stage, side, c],
-            device_id={"reg": d - 1 if to_left else d + 1},
-            device_id_type=pl.DeviceIdType.MESH)
-
-    def start_halo(stage, chunks):
-        @pl.when(d > 0)
-        def _():
-            for c in chunks:
-                halo(stage, True, c).start()
-
-        @pl.when(d < n - 1)
-        def _():
-            for c in chunks:
-                halo(stage, False, c).start()
-
-    def wait_halo(stage, c):
-        @pl.when(d > 0)
-        def _():
-            halo(stage, False, c).wait_recv()
-
-        @pl.when(d < n - 1)
-        def _():
-            halo(stage, True, c).wait_recv()
-
-    def sent_halo(stage, chunks):
-        @pl.when(d > 0)
-        def _():
-            for c in chunks:
-                halo(stage, True, c).wait_send()
-
-        @pl.when(d < n - 1)
-        def _():
-            for c in chunks:
-                halo(stage, False, c).wait_send()
-
-    chunks0 = range(FIRST)
-    chunks1 = range(H - 1 - FIRST)
-    start_halo(0, chunks0)
-
     loads[-1].wait()
 
     def split_shocks(r, _):
@@ -187,34 +190,39 @@
         if keep:
             return out.astype(jnp.bfloat16)
 
-    def several(src, dst, which, j, keep):
+    half = cols // 2
+
+    def several(src, dst, which, j, keep, part):
         def block(i, _):
-            c0 = pl.multiple_of(i * 32, 32)
+            c0 = part * half + i * 16
+            if half != 16:
+                c0 = pl.multiple_of(c0, 16)
             for r in which:
-                kept = piece(src, dst, r, j, keep, pl.ds(c0, 32))
+                kept = piece(src, dst, r, j, keep, pl.ds(c0, 16))
                 if keep:
-                    eb[r - regions, pl.ds(j * cols + c0, 32), :] = kept
+                    eb[r - regions, pl.ds(j * cols + c0, 16), :] = kept
             return 0
 
-        if cols == 32:
+        if half == 16:
             block(0, 0)
         else:
-            lax.fori_loop(0, cols // 32, block, 0)
-
-    def ring(src, dst, c, j):
+            lax.fori_loop(0, half // 16, block, 0)
+
+    def ring(src, dst, c, j, part):
         near = c * REACH
         lo, hi = regions - near - REACH, 2 * regions + near
         several(src, dst, [lo + q for q in range(REACH)] + [hi + q for q in range(REACH)],
-                j, False)
-
-    def inner(src, dst, j, start=0):
+                j, False, part)
+
+    def inner(src, dst, j, part, start=0):
         def one(i, _):
-            several(src, dst, [regions + start + 4 * i + q for q in range(4)], j, True)
+            several(src, dst, [regions + start + 4 * i + q for q in range(4)], j, True, part)
             return 0
         lax.fori_loop(0, (regions - 2 * start) // 4, one, 0)
 
-    def edge(src, dst, j):
-        several(src, dst, [regions, regions + 1, 2 * regions - 2, 2 * regions - 1], j, True)
+    def edge(src, dst, j, part):
+        several(src, dst, [regions, regions + 1, 2 * regions - 2, 2 * regions - 1],
+                j, True, part)
 
     def dots(lo, hi):
         tile = min(256, 2 * length)
@@ -231,27 +239,30 @@
 
     acc[...] = jnp.zeros_like(acc)
     first = [x0, x1, x2, x3, x4]
-    for c in chunks0:
-        wait_halo(0, c)
-        for j in range(1, c + 1):
-            ring(first[j - 1], first[j], c - j, j)
-        if c + 1 < FIRST:
-            inner(first[c], first[c + 1], c + 1)
-        else:
-            edge(first[c], first[c + 1], c + 1)
-            start_halo(1, [0])
-            inner(first[c], first[c + 1], c + 1, REACH)
-            start_halo(1, chunks1[1:])
+    for part in range(2):
+        for c in chunks0:
+            wait_halo(0, c, part)
+            for j in range(1, c + 1):
+                ring(first[j - 1], first[j], c - j, j, part)
+            if c + 1 < FIRST:
+                inner(first[c], first[c + 1], c + 1, part)
+            else:
+                edge(first[c], first[c + 1], c + 1, part)
+                start_halo(1, [0], part)
+                inner(first[c], first[c + 1], c + 1, part, REACH)
+                start_halo(1, chunks1[1:], part)
     dots(0, FIRST + 1)
     second = [x4, x1, x2, x3]
-    for c in chunks1:
-        wait_halo(1, c)
-        for j in range(1, c + 1):
-            ring(second[j - 1], second[j], c - j, FIRST + j)
-        inner(second[c], second[c + 1], FIRST + c + 1)
+    for part in range(2):
+        for c in chunks1:
+            wait_halo(1, c, part)
+            for j in range(1, c + 1):
+                ring(second[j - 1], second[j], c - j, FIRST + j, part)
+            inner(second[c], second[c + 1], FIRST + c + 1, part)
     dots(FIRST + 1, H)
-    sent_halo(0, chunks0)
-    sent_halo(1, chunks1)
+    for part in range(2):
+        sent_halo(0, chunks0, part)
+        sent_halo(1, chunks1, part)
 
     width = 2 * length
     pos = lax.rem(lax.broadcasted_iota(jnp.int32, (cols, width), 1), length)
@@ -339,8 +350,8 @@
             pltpu.VMEM((n // 2, H, 2, width), f32),
             pltpu.VMEM((n // 2, H, 2, width), f32),
             pltpu.SemaphoreType.DMA((10,)),
-            pltpu.SemaphoreType.DMA((2, 2, FIRST)),
-            pltpu.SemaphoreType.DMA((2, 2, FIRST)),
+            pltpu.SemaphoreType.DMA((2, 2, FIRST, 2)),
+            pltpu.SemaphoreType.DMA((2, 2, FIRST, 2)),
             pltpu.SemaphoreType.DMA((2,)),
             pltpu.SemaphoreType.DMA((n // 2,)),
             pltpu.SemaphoreType.DMA((n // 2,)),

time: 29.7 us -> 29.4 us (0.990)
  Pallas kernels: 28.2 us -> 27.9 us
where the time goes in v3:
time: 29.4 us; the launch traced here: 29.2 us
  Pallas kernels  27.9 us (95%)
  local copies, waits for them, and re-layouts  1.32 us (4%)
    pallas_call x1, Pallas kernels, per_device(): pl.pallas_call(functools.partial(kernel, n), out_shape=jax.ShapeDtypeStru...  27.9 us
    unnamed x1, local copies, waits for them, and re-layouts  1.32 us

profile of v3, /device:TPU:0, one launch (start us, length us, event | category | flops | bytes accessed | tf_op | source)
XLA Modules:
  0.0 29.2 jit_solution(9146654578465381169)
XLA Ops:
  0.0 27.9 %jacobian.1 = f32[8,2,2,128]{3,2,1,0:T(2,128)} custom-call(f32[8,16,2,256]{3,2,1,0:T(2,128)} %bitcast.5, bf16[4096,128]{1,0:T(8,128)(2,1)} %bitcast.4, f32[128,256]{1,0:T(8,128)} %lw_hbm.1, s32[128,256]{1,0:T(8,128)} %li_hbm.1, f32[4,128]{1,0:T(4,128)} %bitcast.6, s32[4,128]{1,0:T(4,128)} %bitcast.7), custom_call_target="tpu_custom_call" | custom-call | tf_op jit(solution)/shard_map/jacobian/pallas_call | solution.py:328
  27.9 1.3 %copy.8 = f32[8,2,2,128]{3,2,1,0:T(2,128)} copy(f32[8,2,2,128]{3,2,1,0:T(2,128)} %jacobian.1) | data formatting | bytes 32768
